TPU v7x, 512 devices: a whole 4x4x16 slice. The times are simulated.
512 devices in a mesh: dp: 64 (over y, x, z_hi, core), frame: 8 (over z_lo).
Axes of the slice: x: 4, y: 4, z: 16 (z_hi: 2, z_lo: 8; z = z_hi * 8 + z_lo), core: 2. Of those that a mesh axis runs over, the one named last changes fastest.
Arguments:
- video_tokens: bfloat16 [1024, 8, 32, 1024], P('dp', 'frame'), may hold values from -14 to 14
- pool_weight: bfloat16 [8, 16, 32], P('frame'), may hold values from -1 to 1
- text_states: bfloat16 [1024, 77, 1600], P(('dp', 'frame')), may hold values from -6 to 6
- norm_gain: float32 [1600], replicated, may hold values from 0.5 to 1.5
- lengths: int32 [1024], P(('dp', 'frame')), may hold values from 1 to 77
- cotangent: bfloat16 [1024, 77, 1600], P(('dp', 'frame')), may hold values from -6 to 6
- query_weight: bfloat16 [1600, 896], P('dp'), may hold values from -0.15625 to 0.15625
- key_weight: bfloat16 [1024, 896], P('dp'), may hold values from -0.1875 to 0.1875
- value_weight: bfloat16 [1024, 896], P('dp'), may hold values from -0.1875 to 0.1875
- out_weight: bfloat16 [896, 1600], P('dp'), may hold values from -0.1875 to 0.1875
Outputs:
- grad_text: bfloat16 [1024, 77, 1600], P(('dp', 'frame'))
- grad_pooled: bfloat16 [1024, 128, 1024], P('dp', 'frame')
Inputs may be any that keep to these rules, and one draw needn't show every extreme that they name: `lengths`: text positions at or after a clip's length are padding.
All inputs are finite; a program needn't handle non-finite values.
Results may differ from a plain program's by a relative error of at most 0.02.
The roundings to bfloat16 on the way count: a program that leaves them out, or rounds other values in their place, can miss the bound.
Values may be sent and summed in bfloat16 or wider, within the bound.
A program may use at most 64 MiB of HBM per device.

v0:
```python
import jax
import jax.numpy as jnp
from jax import lax
from jax.sharding import Mesh
from jax.sharding import PartitionSpec as P

HD = 64
DP = ("dp_0", "dp_1", "dp_2", "dp_3")
DP_FRAME = ("dp_0", "dp_1", "dp_2", "dp_3", "frame")


EPSILON = 1e-05


def in_one_piece(arrays, axis, dim, along):
    ends, at = ([], 0)
    for a in arrays[:-1]:
        at += a.shape[along]
        ends.append(at)
    both = jnp.concatenate(arrays, axis=along)
    return tuple(jnp.split(lax.all_gather(both, axis, axis=dim, tiled=True), ends, axis=along))


def cut_along(x, dim, size):
    shape = x.shape
    blocks = x.reshape(*shape[:dim], size, shape[dim] // size, *shape[dim + 1 :])
    return jnp.moveaxis(blocks, dim, 0)


def edges_of(length, count):
    unit = 8 if length >= 8 * count else 1
    return [length // unit * k // count * unit for k in range(1, count)]


def in_order(blocks, dim):
    blocks = jnp.moveaxis(blocks, 0, dim)
    shape = blocks.shape
    return blocks.reshape(*shape[:dim], shape[dim] * shape[dim + 1], *shape[dim + 2 :])


def several_exchanges(x, axis, pieces, split_dim, concat_dim):
    blocks = cut_along(x, split_dim, lax.axis_size(axis))
    split_at = max(range(1, max(2, blocks.ndim - 1)), key=lambda d: blocks.shape[d])
    finished = []
    for section in jnp.split(blocks, edges_of(blocks.shape[split_at], pieces), axis=split_at):
        if section.size:
            finished.append(lax.all_to_all(section, axis, split_axis=0, concat_axis=0, tiled=True))
    return in_order(jnp.concatenate(finished, axis=split_at), concat_dim)


def from_everyone(x, axis):
    size = lax.axis_size(axis)
    return lax.all_to_all(jnp.broadcast_to(x[None], (size, *x.shape)), axis, 0, 0, tiled=True)


def whole_of(x, axes, dim):
    far, near = axes
    leading = from_everyone(x, far)
    blocks = jnp.swapaxes(from_everyone(leading, near), 0, 1)
    return in_order(blocks.reshape(-1, *x.shape), dim)


def product(left, right):
    return jnp.dot(left, right, preferred_element_type=jnp.float32)


def product_back(left, right):
    return lax.dot_general(
        left, right, (((1,), (1,)), ((), ())), preferred_element_type=jnp.float32
    )


def shards(
    video_tokens,
    pool_weight,
    text_states,
    norm_gain,
    lengths,
    cotangent,
    query_weight,
    key_weight,
    value_weight,
    out_weight,
):
    clip_count = video_tokens.shape[0]
    visual_width = video_tokens.shape[3]
    latents_here = video_tokens.shape[1] * pool_weight.shape[1]
    text_clips = text_states.shape[0]
    text_length = text_states.shape[1]
    model_width = text_states.shape[2]
    head_width = query_weight.shape[1]
    head_count = head_width // HD
    score_scale = HD ** (-0.5)
    pooled = jnp.einsum(
        "flp,cfpv->cflv", pool_weight, video_tokens, preferred_element_type=jnp.float32
    )
    pooled = pooled.astype(jnp.bfloat16).reshape(clip_count, latents_here, visual_width)
    query_full = lax.all_gather(query_weight, DP, axis=0, tiled=True)
    key_full, value_full = in_one_piece((key_weight, value_weight), DP, 0, 1)
    moved_pooled = several_exchanges(pooled, "frame", 2, 0, 1)
    flat_rows = moved_pooled.reshape(-1, visual_width)
    key_rows = product(flat_rows, key_full)
    value_rows = product(flat_rows, value_full)
    key_flat = key_rows.astype(jnp.bfloat16)
    value_flat = value_rows.astype(jnp.bfloat16)
    key_latents = key_flat.reshape(text_clips, -1, head_width)
    value_latents = value_flat.reshape(text_clips, -1, head_width)
    latent_total = key_latents.shape[1]
    text_rows = text_states.reshape(-1, model_width).astype(jnp.float32)
    average = jnp.mean(text_rows, axis=1, keepdims=True)
    centered = text_rows - average
    inverse = lax.rsqrt(jnp.mean(centered * centered, axis=1, keepdims=True) + EPSILON)
    unit_rows = centered * inverse
    normed = (unit_rows * norm_gain).astype(jnp.bfloat16)
    queries = product(normed, query_full).astype(jnp.bfloat16)
    query_heads = queries.reshape(text_clips, text_length, head_count, HD)
    key_heads = key_latents.reshape(text_clips, latent_total, head_count, HD)
    value_heads = value_latents.reshape(text_clips, latent_total, head_count, HD)
    scores = (
        jnp.einsum("cthd,clhd->chtl", query_heads, key_heads, preferred_element_type=jnp.float32)
        * score_scale
    )
    row_max = jnp.max(scores, axis=3, keepdims=True)
    shifted = jnp.exp(scores - row_max)
    attn_probs = shifted / jnp.sum(shifted, axis=3, keepdims=True)
    probs_low = attn_probs.astype(jnp.bfloat16)
    attended = jnp.einsum(
        "chtl,clhd->cthd", probs_low, value_heads, preferred_element_type=jnp.float32
    ).astype(jnp.bfloat16)
    positions = lax.broadcasted_iota(jnp.int32, (text_clips, text_length), 1)
    valid_mask = positions < lengths[:, None]
    grad_out = jnp.where(valid_mask[:, :, None], cotangent, jnp.zeros_like(cotangent)).reshape(
        -1, model_width
    )
    grad_att = product_back(
        grad_out, whole_of(out_weight, (("dp_0", "dp_1", "dp_2"), "dp_3"), 0)
    ).astype(jnp.bfloat16)
    grad_heads = grad_att.reshape(text_clips, text_length, head_count, HD)
    grad_probs = jnp.einsum(
        "cthd,clhd->chtl", grad_heads, value_heads, preferred_element_type=jnp.float32
    )
    row_term = jnp.einsum(
        "cthd,cthd->cht", grad_heads.astype(jnp.float32), attended.astype(jnp.float32)
    )[..., None]
    grad_scores = (attn_probs * (grad_probs - row_term) * score_scale).astype(jnp.bfloat16)
    grad_queries = (
        jnp.einsum("chtl,clhd->cthd", grad_scores, key_heads, preferred_element_type=jnp.float32)
        .astype(jnp.bfloat16)
        .reshape(-1, head_width)
    )
    grad_keys = (
        jnp.einsum("chtl,cthd->clhd", grad_scores, query_heads, preferred_element_type=jnp.float32)
        .astype(jnp.bfloat16)
        .reshape(text_clips, latent_total, head_width)
    )
    grad_values = (
        jnp.einsum("chtl,cthd->clhd", probs_low, grad_heads, preferred_element_type=jnp.float32)
        .astype(jnp.bfloat16)
        .reshape(text_clips, latent_total, head_width)
    )
    back_grad_keys = grad_keys.reshape(-1, head_width)
    back_grad_values = grad_values.reshape(-1, head_width)
    result = product_back(back_grad_keys, key_full) + product_back(back_grad_values, value_full)
    local_grad = result.astype(jnp.bfloat16).reshape(text_clips, latent_total, visual_width)
    grad_pooled = lax.all_to_all(local_grad, "frame", split_axis=1, concat_axis=0, tiled=True)
    grad_normed = product_back(grad_queries, query_full)
    scaled_grad = grad_normed * norm_gain
    grad_rows = inverse * (
        scaled_grad
        - jnp.mean(scaled_grad, axis=1, keepdims=True)
        - unit_rows * jnp.mean(scaled_grad * unit_rows, axis=1, keepdims=True)
    )
    grad_text = grad_rows.astype(jnp.bfloat16).reshape(text_clips, text_length, model_width)
    return (grad_text, grad_pooled)


def solution(mesh):
    split = Mesh(
        mesh.devices.reshape(4, 4, 2, 2, mesh.shape["frame"]),
        ("dp_0", "dp_1", "dp_2", "dp_3", "frame"),
    )
    return jax.shard_map(
        shards,
        mesh=split,
        in_specs=(
            P(DP, "frame", None, None),
            P("frame", None, None),
            P(DP_FRAME, None, None),
            P(),
            P(DP_FRAME),
            P(DP_FRAME, None, None),
            P(DP, None),
            P(DP, None),
            P(DP, None),
            P(DP, None),
        ),
        out_specs=(P(DP_FRAME, None, None), P(DP, "frame", None)),
        check_vma=False,
    )
```

profile of v0, /device:TPU:1, one launch (start us, length us, event | category | flops | bytes accessed | tf_op | source)
XLA Modules:
  0.0 374.1 jit_solution(13311326091316773461)
XLA Ops:
  10.1 25.1 %all_to_all.38 = bf16[8,2,8,1024]{3,2,1,0:T(8,128)(2,1)S(1)} all-to-all(bf16[8,2,8,1024]{3,2,1,0:T(8,128)(2,1)S(1)} %get-tuple-element.15), channel_id=1, replica_groups=mesh['dp_0'=4,'dp_1'=4,'dp_2'=2,'dp_3'=2,'frame'=8] {'frame'}, dimensions={0} | all-to-all | bytes 524288 | tf_op jit(solution)/shard_map/all_to_all | solution.py:47
  35.2 9.1 %all-to-all-start = ((bf16[8,2,8,1024]{3,2,1,0:T(8,128)(2,1)}), bf16[8,2,8,1024]{3,2,1,0:T(8,128)(2,1)S(1)}, u32[]{:S(2)}, u32[]{:S(2)}) async-start(bf16[8,2,8,1024]{3,2,1,0:T(8,128)(2,1)} %get-tuple-element.14), calls=%async_computation | async-start | bytes 524288 | tf_op jit(solution)/shard_map/all_to_all | solution.py:47
  45.1 11.0 %all-to-all-done = bf16[8,2,8,1024]{3,2,1,0:T(8,128)(2,1)S(1)} async-done(((bf16[8,2,8,1024]{3,2,1,0:T(8,128)(2,1)}), bf16[8,2,8,1024]{3,2,1,0:T(8,128)(2,1)S(1)}, u32[]{:S(2)}, u32[]{:S(2)}) %all-to-all-start) | async-done | bytes 262176 | tf_op jit(solution)/shard_map/all_to_all | solution.py:47
  58.2 13.0 %all-to-all-start.2 = ((bf16[32,14,1600]{2,1,0:T(8,128)(2,1)}), bf16[32,14,1600]{2,1,0:T(8,128)(2,1)}, u32[]{:S(2)}, u32[]{:S(2)}) async-start(bf16[32,14,1600]{2,1,0:T(8,128)(2,1)} %broadcast_in_dim.16), calls=%async_computation.2 | async-start | bytes 3407872 | tf_op jit(solution)/shard_map/all_to_all | solution.py:53
  77.0 31.6 %all-to-all-done.2 = bf16[32,14,1600]{2,1,0:T(8,128)(2,1)} async-done(((bf16[32,14,1600]{2,1,0:T(8,128)(2,1)}), bf16[32,14,1600]{2,1,0:T(8,128)(2,1)}, u32[]{:S(2)}, u32[]{:S(2)}) %all-to-all-start.2) | async-done | bytes 1433632 | tf_op jit(solution)/shard_map/all_to_all | solution.py:53
  110.6 18.8 %all_to_all.39 = bf16[2,32,14,1600]{3,1,2,0:T(8,128)(2,1)S(1)} all-to-all(bf16[2,32,14,1600]{3,1,2,0:T(8,128)(2,1)S(1)} %broadcast_in_dim.17), channel_id=1, replica_groups=mesh['dp_0'=4,'dp_1'=4,'dp_2'=2,'dp_3'=2,'frame'=8] {'dp_3'}, dimensions={0} | all-to-all | bytes 5734400 | tf_op jit(solution)/shard_map/all_to_all | solution.py:53
  129.3 2.8 copy.99
  132.1 5.7 %reshape_reshape.24 = bf16[896,1600]{1,0:T(8,128)(2,1)} reshape(bf16[32,2,14,1600]{3,2,1,0:T(8,128)(2,1)} %copy.99) | data formatting | bytes 5734400 | tf_op jit(solution)/shard_map/reshape;reshape | solution.py:38
  137.8 2.9 convolution_convert_fusion.5
  143.7 2.7 copy.118
  146.4 47.1 %all-gather.6.cloned.1.call-done = bf16[64,25,896]{2,1,0:T(8,128)(2,1)} async-done(((bf16[1,25,896]{2,1,0:T(8,128)(2,1)}), bf16[64,25,896]{2,1,0:T(8,128)(2,1)}) %all-gather.6.cloned.1.call-update) | async-done | bytes 2867216 | tf_op jit(solution)/shard_map/all_gather | solution.py:98
  193.5 4.6 %reshape.108 = bf16[1600,896]{1,0:T(8,128)(2,1)} reshape(bf16[64,25,896]{2,1,0:T(8,128)(2,1)} %all-gather.6.cloned.1.call-done) | data formatting | bytes 5734400
  198.2 2.6 convolution_convert_fusion.6
  202.6 111.6 %all-gather.4.cloned.1.call-done = bf16[1024,1792]{1,0:T(8,128)(2,1)} async-done(((bf16[16,1792]{1,0:T(8,128)(2,1)}), bf16[1024,1792]{1,0:T(8,128)(2,1)}) %all-gather.4.cloned.1.call-update) | async-done | bytes 3670032 | tf_op jit(solution)/shard_map/all_gather | solution.py:21
  314.3 3.0 fusion.20
  317.2 1.8 reshape.113
  320.5 3.2 fusion.23
  327.0 2.2 fusion.49
  329.3 2.0 fusion.32
  332.3 2.2 fusion.16
  339.2 4.1 %all-to-all-start.4 = ((bf16[2,128,1024]{2,0,1:T(2,128)(2,1)}), bf16[2,128,1024]{2,0,1:T(2,128)(2,1)}, u32[]{:S(2)}, u32[]{:S(2)}) async-start(bf16[2,128,1024]{2,0,1:T(2,128)(2,1)} %copy.110), calls=%async_computation.4 | async-start | bytes 1048576 | tf_op jit(solution)/shard_map/all_to_all | solution.py:165
  346.7 3.0 fusion.47
  351.5 13.9 %all-to-all-done.4 = bf16[2,128,1024]{2,0,1:T(2,128)(2,1)} async-done(((bf16[2,128,1024]{2,0,1:T(2,128)(2,1)}), bf16[2,128,1024]{2,0,1:T(2,128)(2,1)}, u32[]{:S(2)}, u32[]{:S(2)}) %all-to-all-start.4) | async-done | bytes 524320 | tf_op jit(solution)/shard_map/all_to_all | solution.py:165
  365.4 2.0 copy.111
  (90 shorter events, 33.7 us)
Async XLA Ops:
  7.2 1.2 copy-start
  7.2 186.3 %all-gather.6.cloned.1.call-start = ((), (), s32[]{:S(2)}) async-start(), calls=%async_computation.6 | async-start | bytes 3727360 | tf_op jit(solution)/shard_map/all_gather | solution.py:98
  9.4 35.0 %copy-start.13 = (bf16[16,896]{1,0:T(8,128)(2,1)S(1)}, bf16[16,896]{1,0:T(8,128)(2,1)}, u32[]{:S(2)}) copy-start(bf16[16,896]{1,0:T(8,128)(2,1)} %param.18) | copy-start | bytes 86020
  9.4 35.0 %copy-start.14 = (bf16[16,896]{1,0:T(8,128)(2,1)S(1)}, bf16[16,896]{1,0:T(8,128)(2,1)}, u32[]{:S(2)}) copy-start(bf16[16,896]{1,0:T(8,128)(2,1)} %param.17) | copy-start | bytes 86020
  9.4 47.4 %copy-start.10 = (bf16[14,1600]{1,0:T(8,128)(2,1)S(1)}, bf16[14,1600]{1,0:T(8,128)(2,1)}, u32[]{:S(2)}) copy-start(bf16[14,1600]{1,0:T(8,128)(2,1)} %param.19) | copy-start | bytes 134404
  35.2 20.9 %all-to-all-start = ((bf16[8,2,8,1024]{3,2,1,0:T(8,128)(2,1)}), bf16[8,2,8,1024]{3,2,1,0:T(8,128)(2,1)S(1)}, u32[]{:S(2)}, u32[]{:S(2)}) async-start(bf16[8,2,8,1024]{3,2,1,0:T(8,128)(2,1)} %get-tuple-element.14), calls=%async_computation | async-start | bytes 524288 | tf_op jit(solution)/shard_map/all_to_all | solution.py:47
  44.3 269.9 %all-gather.4.cloned.1.call-start = ((), (), s32[]{:S(2)}) async-start(), calls=%async_computation.5 | async-start | bytes 3727360 | tf_op jit(solution)/shard_map/all_gather | solution.py:21
  58.2 13.0 %copy-start.1 = (bf16[2,77,1600]{2,0,1:T(2,128)(2,1)S(1)}, bf16[2,77,1600]{2,0,1:T(2,128)(2,1)}, u32[]{:S(2)}) copy-start(bf16[2,77,1600]{2,0,1:T(2,128)(2,1)} %param.12) | copy-start | bytes 1478404
  58.2 50.4 %all-to-all-start.2 = ((bf16[32,14,1600]{2,1,0:T(8,128)(2,1)}), bf16[32,14,1600]{2,1,0:T(8,128)(2,1)}, u32[]{:S(2)}, u32[]{:S(2)}) async-start(bf16[32,14,1600]{2,1,0:T(8,128)(2,1)} %broadcast_in_dim.16), calls=%async_computation.2 | async-start | bytes 3407872 | tf_op jit(solution)/shard_map/all_to_all | solution.py:53
  72.9 125.3 %copy-start.15 = (f32[154]{0:T(256)}, f32[154]{0:T(256)S(1)}, u32[]{:S(2)}) copy-start(f32[154]{0:T(256)S(1)} %rsqrt.12) | copy-start | bytes 1852
  73.4 124.8 %copy-start.17 = (f32[154]{0:T(256)}, f32[154]{0:T(256)S(1)}, u32[]{:S(2)}) copy-start(f32[154]{0:T(256)S(1)} %div.24) | copy-start | bytes 1852
  146.4 51.8 %copy-start.11 = (f32[1600]{0:T(1024)S(1)}, f32[1600]{0:T(1024)}, u32[]{:S(2)}) copy-start(f32[1600]{0:T(1024)} %param.13) | copy-start | bytes 19204
  200.8 113.5 %copy-start.7 = (bf16[8,2,16,1024]{3,2,0,1:T(8,128)(2,1)S(1)}, bf16[8,2,16,1024]{3,2,0,1:T(8,128)(2,1)}, u32[]{:S(2)}) copy-start(bf16[8,2,16,1024]{3,2,0,1:T(8,128)(2,1)} %copy.119) | copy-start | bytes 1572868
  329.2 2.0 copy-start.4
  329.2 2.0 copy-start.6
  329.3 2.0 copy-start.9
  331.3 1.0 copy-start.8
  332.3 4.0 %copy-start.20 = (bf16[1024,1792]{1,0:T(8,128)(2,1)S(1)}, bf16[1024,1792]{1,0:T(8,128)(2,1)}, u32[]{:S(2)}) copy-start(bf16[1024,1792]{1,0:T(8,128)(2,1)} %all-gather.4.cloned.1.call-done) | copy-start | bytes 11010052
  334.5 1.0 copy-start.3
  337.9 5.5 %copy-start.2 = (bf16[2,128,14,64]{1,3,2,0:T(8,128)(2,1)S(1)}, bf16[2,128,14,64]{1,3,2,0:T(8,128)(2,1)}, u32[]{:S(2)}) copy-start(bf16[2,128,14,64]{1,3,2,0:T(8,128)(2,1)} %copy.104) | copy-start | bytes 1376260
  339.2 26.1 %all-to-all-start.4 = ((bf16[2,128,1024]{2,0,1:T(2,128)(2,1)}), bf16[2,128,1024]{2,0,1:T(2,128)(2,1)}, u32[]{:S(2)}, u32[]{:S(2)}) async-start(bf16[2,128,1024]{2,0,1:T(2,128)(2,1)} %copy.110), calls=%async_computation.4 | async-start | bytes 1048576 | tf_op jit(solution)/shard_map/all_to_all | solution.py:165
  344.6 2.1 copy-start.12
  344.6 2.1 copy-start.16
  344.6 2.1 copy-start.18
  (2 other events, 1.4 us)
Sparse Core Ops, SparseCore 0:
  12.3 181.1 all-gather.5
  197.8 116.3 all-gather.3
where the time goes:
time: 380 us; the launch traced here: 374 us
  waiting for transfers between devices  216 us (57%)
  blocking collectives  43.8 us (12%)
  local copies, waits for them, and re-layouts  41.6 us (11%)
  starting transfers between devices  26.4 us (7%)
  matrix products  25.7 us (7%)
  between operations  14.5 us (4%)
  other arithmetic  6.19 us (2%)
    all_gather x1, waiting for transfers between devices, in_one_piece(): lax.all_gather(both, axis, axis=dim, tiled=True)  112 us
    all_gather x1, waiting for transfers between devices, shards(): query_full = lax.all_gather(query_weight, DP, axis=0, tiled=True)  47.1 us
    all_to_all x1, waiting for transfers between devices, from_everyone(): lax.all_to_all(jnp.broadcast_to(x[None], (size, *x.shape)), axis, 0, 0, t...  31.6 us
    all_to_all x1, blocking collectives, several_exchanges(): lax.all_to_all(section, axis, split_axis=0, concat_axis=0, tiled=True)  25.1 us
    all_to_all x1, blocking collectives, from_everyone(): lax.all_to_all(jnp.broadcast_to(x[None], (size, *x.shape)), axis, 0, 0, t...  18.8 us
    all_to_all x1, waiting for transfers between devices, shards(): lax.all_to_all(local_grad, 'frame', split_axis=1, concat_axis=0, tiled=True)  13.9 us
    all_to_all x1, starting transfers between devices, from_everyone(): lax.all_to_all(jnp.broadcast_to(x[None], (size, *x.shape)), axis, 0, 0, t...  13 us
    unnamed x47, local copies, waits for them, and re-layouts  11.1 us
  transfers between devices with their start and end apart: 5, of which 5 were waited for; matrix products, arithmetic and copies ran while one was open for 12% of the time, Pallas kernels for 0%

commit v1 on v0

v1 whole, which is shorter than its diff:
```python
import functools

import jax
import jax.numpy as jnp
from jax import lax
from jax.experimental import pallas as pl
from jax.experimental.pallas import tpu as pltpu
from jax.sharding import PartitionSpec as P

HD = 64
EPSILON = 1e-05
MESH = pl.DeviceIdType.MESH
F32 = jnp.float32
BF16 = jnp.bfloat16

D = 1600
DP = 1664
V = 1024
HW = 896
TEXT = 77
TP = 80
QL = 1408
LAT = 16
FRAMES = 8
ROWS = 2 * TP


def dot(left, right):
    return jnp.dot(left, right, preferred_element_type=F32)


def dot_nt(left, right):
    return lax.dot_general(left, right, (((1,), (1,)), ((), ())), preferred_element_type=F32)


def dot_tn(left, right):
    return lax.dot_general(left, right, (((0,), (0,)), ((), ())), preferred_element_type=F32)


def kernel(
    video, pool_w, text, gain_in, lengths, cot, q_in, k_in, v_in, o_in,
    grad_text, grad_pooled,
    qb, ob, kb, vb, qw, ow, qf, of, qs, os_, xs, cs, gain, unit, normed, go, queries, ga,
    pooled, lat, kl, vl, gk, gv, gq, back,
    send, recv, cross_send, cross_recv, pool_send, pool_recv, back_send, back_recv, own_sem,
):
    dp = lax.axis_index("dp")
    f = lax.axis_index("frame")
    y, x, h, c = dp // 16, (dp // 4) % 4, (dp // 2) % 2, dp % 2
    o = 1 - h

    def device(y, x, h, c, f):
        return (((y * 4 + x) * 2 + h) * 2 + c, f)

    def up(i):
        return (i + 1) % 4

    def down(i):
        return (i + 3) % 4

    def far(i):
        return (i + 2) % 4

    sibling = device(y, x, h, 1 - c, f)
    x_up, x_down = device(y, up(x), h, c, f), device(y, down(x), h, c, f)
    y_up, y_down = device(up(y), x, h, c, f), device(down(y), x, h, c, f)

    barrier = pltpu.get_barrier_semaphore()

    def greet(who):
        pl.semaphore_signal(barrier, inc=1, device_id=who, device_id_type=MESH)

    for who in (sibling, x_up, x_down, y_up, y_down):
        greet(who)
    for step in range(1, FRAMES):
        greet((dp, (f + step) % FRAMES))
    other_dp = device(y, x, o, c, f)[0]
    at_low = f == 0
    at_high = f == FRAMES - 1
    at_end = jnp.logical_or(at_low, at_high)

    @pl.when(at_low)
    def _():
        for k in range(4):
            greet((other_dp, 7 - k))

    @pl.when(at_high)
    def _():
        for k in range(4):
            greet((other_dp, k))

    @pl.when(jnp.logical_not(at_end))
    def _():
        greet((other_dp, jnp.where(f < 4, FRAMES - 1, 0)))

    qs[...] = jnp.zeros_like(qs)
    q = q_in[...].astype(F32)
    qs[:, 0:HW] = q[0:16]
    qs[0:8, HW:QL] = q[16:24, 0:512]
    qs[8:16, HW:HW + 384] = q[16:24, 512:HW]
    for b in range(7):
        qs[8 + b:9 + b, HW + 384:QL] = q[24:25, 128 * b:128 * b + 128]
    qb[y, x, h, c] = qs[...].astype(BF16)
    os_[...] = jnp.zeros_like(os_)
    os_[0:14, 0:D] = o_in[...].astype(F32)
    ob[y, x, h, c] = os_[...].astype(BF16)
    kb[y, x, h, c] = k_in[...]
    vb[y, x, h, c] = v_in[...]

    i0 = lax.broadcasted_iota(jnp.int32, (32, 256), 0)
    i1 = lax.broadcasted_iota(jnp.int32, (32, 256), 1)
    spread = jnp.where(i1 % 32 == i0, 1.0, 0.0).astype(BF16)
    wide = dot(pool_w[...], spread)
    wide = jnp.concatenate([wide] * 8, axis=0)
    j0 = lax.broadcasted_iota(jnp.int32, (128, 256), 0)
    j1 = lax.broadcasted_iota(jnp.int32, (128, 256), 1)
    diag = jnp.where(j0 // 16 == j1 // 32, wide, 0.0).astype(BF16)
    for half in range(2):
        part = dot(diag, video[256 * half:256 * half + 256, :])
        pooled[128 * half:128 * half + 128, :] = part.astype(BF16)

    count = 12 + jnp.where(at_end, 4, 1)
    pl.semaphore_wait(barrier, count)

    bufs = (qb, ob, kb, vb)
    x_first = (True, False, True, False)
    sends = []

    def copy(src, dst, s_sem, r_sem, who):
        return pltpu.make_async_remote_copy(
            src_ref=src, dst_ref=dst, send_sem=s_sem, recv_sem=r_sem, device_id=who,
            device_id_type=MESH)

    def parts(w):
        buf = bufs[w]
        if x_first[w]:
            return (
                lambda a, z: buf.at[y, a, z, c],
                lambda b, z: buf.at[b, :, z, c],
                lambda b, z, k: buf.at[b, pl.ds(2 * k, 2), z, c],
                (lambda b, z: buf.at[b, :, z, 1 - c]),
                x, y, x_up, x_down, y_up, y_down,
            )
        return (
            lambda a, z: buf.at[a, x, z, c],
            lambda b, z: buf.at[:, b, z, c],
            lambda b, z, k: buf.at[pl.ds(2 * k, 2), b, z, c],
            (lambda b, z: buf.at[:, b, z, 1 - c]),
            y, x, y_up, y_down, x_up, x_down,
        )

    def step(w, s, k):
        item, row, pair, other_row, a, b, a_up, a_down, b_up, b_down = parts(w)
        z = h if s == 0 else o

        def go_(ref, index, who):
            moving = copy(ref, ref, send.at[w, s, index], recv.at[w, s, index], who)
            moving.start()
            sends.append(moving)

        def come(ref, index, who):
            copy(ref, ref, send.at[w, s, index], recv.at[w, s, index], who).wait_recv()

        if k == 0:
            if s == 1:
                mine = bufs[w].at[y, x, o, c]
                copy(mine, mine, cross_send.at[w, 0], cross_recv.at[w], (other_dp, f)).wait_recv()
            go_(item(a, z), 0, a_up)
            go_(item(a, z), 1, a_down)
        elif k == 1:
            if s == 0:
                come(item(down(a), z), 0, a_up)
                go_(item(down(a), z), 2, a_up)
                come(item(up(a), z), 1, a_down)
            else:
                come(item(up(a), z), 1, a_down)
                go_(item(up(a), z), 2, a_down)
                come(item(down(a), z), 0, a_up)
        elif k == 2:
            come(item(far(a), z), 2, a_up if s == 0 else a_down)
            go_(pair(b, z, 0), 3, b_up)
            go_(pair(b, z, 1), 6, b_down)
            go_(pair(b, z, 1), 4, b_up)
            go_(pair(b, z, 0), 5, b_down)
            go_(row(b, z), 9, sibling)
        elif k == 3:
            come(pair(down(b), z, 0), 3, b_up)
            go_(pair(down(b), z, 0), 7, b_up)
            come(pair(up(b), z, 1), 6, b_down)
            go_(pair(up(b), z, 1), 8, b_down)
            come(pair(down(b), z, 1), 4, b_up)
            go_(row(down(b), z), 10, sibling)
            come(pair(up(b), z, 0), 5, b_down)
            go_(row(up(b), z), 11, sibling)
        elif k == 4:
            come(pair(far(b), z, 0), 7, b_up)
            come(pair(far(b), z, 1), 8, b_down)
            go_(row(far(b), z), 12, sibling)
        else:
            for n, at in enumerate((b, down(b), up(b), far(b))):
                ref = other_row(at, z)
                copy(ref, ref, send.at[w, s, 9 + n], recv.at[w, s, 9 + n], sibling).wait_recv()

    units = ((0, 1, 0), (0, 1, 1), (2, 3, 0), (2, 3, 1))

    def round_(r):
        for u, (w0, w1, s) in enumerate(units):
            k = r - u
            if 0 <= k <= 4:
                step(w0, s, k)
                step(w1, s, k)

    round_(0)

    def cross(where, k, w, target):
        mine = bufs[w].at[y, x, h, c]
        return copy(mine, mine, cross_send.at[w, k], cross_recv.at[w], (other_dp, target))

    @pl.when(at_low)
    def _():
        for w in range(4):
            for k in range(4):
                cross(0, k, w, 4 + k).start()

    @pl.when(at_high)
    def _():
        for w in range(4):
            for k in range(4):
                cross(1, k, w, 3 - k).start()

    def pool_copy(clip, to, frm):
        start = pl.multiple_of(32 * to + 16 * clip, 16)
        place = pl.multiple_of(16 * frm, 16)
        return copy(
            pooled.at[pl.ds(start, 16), :], lat.at[clip, pl.ds(place, 16), :],
            pool_send.at[clip, to], pool_recv.at[clip, frm], (dp, to))

    for clip in range(2):
        for n in range(1, FRAMES):
            pool_copy(clip, (f + n) % FRAMES, f).start()
        start = pl.multiple_of(32 * f + 16 * clip, 16)
        place = pl.multiple_of(16 * f, 16)
        lat[clip, pl.ds(place, 16), :] = pooled[pl.ds(start, 16), :]

    gain[...] = jnp.zeros_like(gain)
    gain[0:1, 0:D] = gain_in[...]
    xs[...] = jnp.zeros_like(xs)
    cs[...] = jnp.zeros_like(cs)
    for clip in range(2):
        xs[TP * clip:TP * clip + TEXT, 0:D] = text[clip].astype(F32)
        cs[TP * clip:TP * clip + TEXT, 0:D] = cot[clip].astype(F32)
    round_(1)
    lane = lax.broadcasted_iota(jnp.int32, (TP, DP), 1)
    position = lax.broadcasted_iota(jnp.int32, (TP, DP), 0)
    inverses = []
    for clip in range(2):
        rows = slice(TP * clip, TP * clip + TP)
        states = xs[rows, :]
        average = jnp.sum(states, axis=1, keepdims=True) * (1.0 / D)
        centered = jnp.where(lane < D, states - average, 0.0)
        square = jnp.sum(centered * centered, axis=1, keepdims=True) * (1.0 / D)
        inverse = lax.rsqrt(square + EPSILON)
        inverses.append(inverse)
        unit_rows = centered * inverse
        unit[rows, :] = unit_rows
        normed[rows, :] = (unit_rows * gain[0:1, :]).astype(BF16)
        go[rows, :] = jnp.where(position < lengths[clip], cs[rows, :], 0.0).astype(BF16)
    round_(2)
    round_(3)
    round_(4)
    round_(5)

    qw[D:DP, :] = jnp.zeros((DP - D, HW), BF16)
    for s in range(2):
        for w in range(2):
            step(w, s, 5)

    def unpack(j, carry):
        for k in range(16):
            xx, zz, cc = k // 4, (k // 2) % 2, k % 2
            t = qb[j, xx, zz, cc].astype(F32)
            at = 25 * k
            qf[at:at + 16, :] = t[:, 0:HW]
            qf[at + 16:at + 24, 0:512] = t[0:8, HW:QL]
            qf[at + 16:at + 24, 512:HW] = t[8:16, HW:HW + 384]
            for b in range(7):
                qf[at + 24:at + 25, 128 * b:128 * b + 128] = t[8 + b:9 + b, HW + 384:QL]
            u = ob[j, xx, zz, cc].astype(F32)
            of[14 * k:14 * k + 14, :] = u[0:14]
        qw[pl.ds(pl.multiple_of(400 * j, 16), 400), :] = qf[...].astype(BF16)
        ow[pl.ds(pl.multiple_of(224 * j, 16), 224), :] = of[...].astype(BF16)
        return carry

    lax.fori_loop(0, 4, unpack, 0)
    queries[...] = dot(normed[...], qw[...]).astype(BF16)
    ga[...] = dot_nt(go[...], ow[...]).astype(BF16)
    round_(6)
    round_(7)
    for s in range(2):
        for w in range(2, 4):
            step(w, s, 5)

    for clip in range(2):
        for n in range(1, FRAMES):
            frm = (f + n) % FRAMES
            place = pl.multiple_of(16 * frm, 16)
            got = lat.at[clip, pl.ds(place, 16), :]
            copy(got, got, pool_send.at[clip, frm], pool_recv.at[clip, frm], (dp, frm)).wait_recv()

    key_w = kb[...].reshape(V, HW)
    value_w = vb[...].reshape(V, HW)
    flat = lat[...].reshape(256, V)
    kl[...] = dot(flat, key_w).astype(BF16)
    vl[...] = dot(flat, value_w).astype(BF16)

    low = lax.broadcasted_iota(jnp.int32, (128, 128), 1) < HD
    scale = HD ** -0.5
    zero = jnp.zeros((128, 128), BF16)

    def split(block):
        return jnp.concatenate([jnp.where(low, block, zero), jnp.where(low, zero, block)], axis=0)

    def back_copy(clip, to, frm):
        rows = pl.multiple_of(16 * to, 16)
        return copy(
            back.at[clip, pl.ds(rows, 16), :], grad_pooled.at[2 * frm + clip],
            back_send.at[clip, to], back_recv.at[clip, frm], (dp, to))

    for clip in range(2):
        rows = slice(TP * clip, TP * clip + TP)
        lats = slice(128 * clip, 128 * clip + 128)
        for p in range(7):
            cols = slice(128 * p, 128 * p + 128)
            qp = queries[rows, cols]
            gp = ga[rows, cols]
            kd = split(kl[lats, cols])
            vd = split(vl[lats, cols])
            scores = dot_nt(kd, qp).reshape(2, 128, TP) * scale
            grad_probs = dot_nt(vd, gp).reshape(2, 128, TP)
            top = jnp.max(scores, axis=1, keepdims=True)
            shifted = jnp.exp(scores - top)
            probs = shifted / jnp.sum(shifted, axis=1, keepdims=True)
            probs_low = probs.astype(BF16)
            row_term = jnp.sum(probs_low.astype(F32) * grad_probs, axis=1, keepdims=True)
            grad_scores = (probs * (grad_probs - row_term) * scale).astype(BF16).reshape(256, TP)
            dk = dot(grad_scores, qp)
            dv = dot(probs_low.reshape(256, TP), gp)
            gk[lats, cols] = jnp.where(low, dk[0:128], dk[128:256]).astype(BF16)
            gv[lats, cols] = jnp.where(low, dv[0:128], dv[128:256]).astype(BF16)
            gq[rows, cols] = dot_tn(grad_scores, kd).astype(BF16)
        result = dot_nt(gk[lats, :], key_w) + dot_nt(gv[lats, :], value_w)
        back[clip] = result.astype(BF16)
        for n in range(1, FRAMES):
            back_copy(clip, (f + n) % FRAMES, f).start()
        mine = pl.multiple_of(16 * f, 16)
        pltpu.make_async_copy(
            back.at[clip, pl.ds(mine, 16), :], grad_pooled.at[2 * f + clip], own_sem.at[clip]
        ).start()

    grad_normed = dot_nt(gq[...], qw[...])
    for clip in range(2):
        rows = slice(TP * clip, TP * clip + TP)
        g = grad_normed[rows] * gain[0:1, :]
        unit_rows = unit[rows, :]
        mean_g = jnp.sum(g, axis=1, keepdims=True) * (1.0 / D)
        mean_gu = jnp.sum(g * unit_rows, axis=1, keepdims=True) * (1.0 / D)
        out = inverses[clip] * (g - mean_g - unit_rows * mean_gu)
        grad_text[clip] = out[0:TEXT, 0:D].astype(BF16)

    for moving in sends:
        moving.wait_send()
    for clip in range(2):
        for n in range(1, FRAMES):
            to = (f + n) % FRAMES
            pool_copy(clip, to, f).wait_send()
            back_copy(clip, to, f).wait_send()
        for n in range(1, FRAMES):
            frm = (f + n) % FRAMES
            got = grad_pooled.at[2 * frm + clip]
            copy(got, got, back_send.at[clip, frm], back_recv.at[clip, frm], (dp, frm)).wait_recv()
        mine = pl.multiple_of(16 * f, 16)
        pltpu.make_async_copy(
            back.at[clip, pl.ds(mine, 16), :], grad_pooled.at[2 * f + clip], own_sem.at[clip]
        ).wait()

    @pl.when(at_low)
    def _():
        for w in range(4):
            for k in range(4):
                cross(0, k, w, 4 + k).wait_send()

    @pl.when(at_high)
    def _():
        for w in range(4):
            for k in range(4):
                cross(1, k, w, 3 - k).wait_send()


def shards(video, pool_w, text, gain, lengths, cot, q_w, k_w, v_w, o_w):
    vmem = pl.BlockSpec(memory_space=pltpu.VMEM)
    smem = pl.BlockSpec(memory_space=pltpu.SMEM)
    dma = pltpu.SemaphoreType.DMA
    return pl.pallas_call(
        kernel,
        out_shape=(
            jax.ShapeDtypeStruct((2, TEXT, D), BF16),
            jax.ShapeDtypeStruct((16, LAT, V), BF16),
        ),
        in_specs=[vmem, vmem, vmem, vmem, smem, vmem, vmem, vmem, vmem, vmem],
        out_specs=(vmem, pl.BlockSpec(memory_space=pl.ANY)),
        scratch_shapes=[
            pltpu.VMEM((4, 4, 2, 2, 16, QL), BF16),
            pltpu.VMEM((4, 4, 2, 2, 16, DP), BF16),
            pltpu.VMEM((4, 4, 2, 2, 16, HW), BF16),
            pltpu.VMEM((4, 4, 2, 2, 16, HW), BF16),
            pltpu.VMEM((DP, HW), BF16),
            pltpu.VMEM((HW, DP), BF16),
            pltpu.VMEM((400, HW), F32),
            pltpu.VMEM((224, DP), F32),
            pltpu.VMEM((16, QL), F32),
            pltpu.VMEM((16, DP), F32),
            pltpu.VMEM((ROWS, DP), F32),
            pltpu.VMEM((ROWS, DP), F32),
            pltpu.VMEM((8, DP), F32),
            pltpu.VMEM((ROWS, DP), F32),
            pltpu.VMEM((ROWS, DP), BF16),
            pltpu.VMEM((ROWS, DP), BF16),
            pltpu.VMEM((ROWS, HW), BF16),
            pltpu.VMEM((ROWS, HW), BF16),
            pltpu.VMEM((256, V), BF16),
            pltpu.VMEM((2, 128, V), BF16),
            pltpu.VMEM((256, HW), BF16),
            pltpu.VMEM((256, HW), BF16),
            pltpu.VMEM((256, HW), BF16),
            pltpu.VMEM((256, HW), BF16),
            pltpu.VMEM((ROWS, HW), BF16),
            pltpu.VMEM((2, 128, V), BF16),
            dma((4, 2, 13)),
            dma((4, 2, 13)),
            dma((4, 4)),
            dma((4,)),
            dma((2, FRAMES)),
            dma((2, FRAMES)),
            dma((2, FRAMES)),
            dma((2, FRAMES)),
            dma((2,)),
        ],
        compiler_params=pltpu.CompilerParams(
            collective_id=0, has_side_effects=True, vmem_limit_bytes=52 * 1024 * 1024
        ),
    )(
        video.reshape(512, V), pool_w.reshape(LAT, 32), text, gain.reshape(1, D), lengths, cot,
        q_w, k_w, v_w, o_w,
    )


def solution(mesh):
    both = ("dp", "frame")
    return jax.shard_map(
        shards,
        mesh=mesh,
        in_specs=(
            P("dp", "frame", None, None), P("frame", None, None), P(both, None, None), P(), P(both),
            P(both, None, None), P("dp", None), P("dp", None), P("dp", None), P("dp", None),
        ),
        out_specs=(P(both, None, None), P("dp", "frame", None)),
        check_vma=False,
    )
```

time: 380 us -> 94.2 us (0.25); the launches traced: 374 us -> 94 us
  waiting for transfers between devices: 216 us -> 0 us
  Pallas kernels: 0 us -> 88.5 us
  blocking collectives: 43.8 us -> 0 us
  local copies, waits for them, and re-layouts: 41.6 us -> 4.74 us
  starting transfers between devices: 26.4 us -> 0 us
  matrix products: 25.7 us -> 0 us
  between operations: 14.5 us -> 0.69 us
  other arithmetic: 6.19 us -> 0 us
    all_gather x2 -> x0, waiting for transfers between devices: 159 us -> none  [the longest x1 112 us: in_one_piece(): lax.all_gather(both, axis, axis=dim, tiled=True)]
    pallas_call x0 -> x1, Pallas kernels: none -> 88.5 us  [shards(): pl.pallas_call(kernel, out_shape=(jax.ShapeDtypeStruct((2, TEXT, D), BF16...]
    all_to_all x3 -> x0, waiting for transfers between devices: 56.5 us -> none  [the longest x1 31.6 us: from_everyone(): lax.all_to_all(jnp.broadcast_to(x[None], (size, *x.shape)), axis, 0, 0, t...]
    all_to_all x2 -> x0, blocking collectives: 43.8 us -> none  [the longest x1 25.1 us: several_exchanges(): lax.all_to_all(section, axis, split_axis=0, concat_axis=0, tiled=True)]
    all_to_all x3 -> x0, starting transfers between devices: 26.3 us -> none  [the longest x1 13 us: from_everyone(): lax.all_to_all(jnp.broadcast_to(x[None], (size, *x.shape)), axis, 0, 0, t...]
    dot_general x13 -> x0, matrix products: 23.5 us -> none  [the longest x3 8.76 us: product(): return jnp.dot(left, right, preferred_element_type=jnp.float32)]
    another operation x5 -> x0, local copies, waits for them, and re-layouts: 12.3 us -> none  [the longest x1 5.7 us: in_order(): blocks.reshape(*shape[:dim], shape[dim] * shape[dim + 1], *shape[dim + 2:])]
    unnamed x47 -> x17, local copies, waits for them, and re-layouts: 11.1 us -> 2.86 us
  transfers between devices with their start and end apart: 5 -> 0, of which waited for: 5 -> 0; matrix products, arithmetic and copies ran while one was open for 12% -> 0% of each run, Pallas kernels for 0% -> 0%
where the time goes in v1:
time: 94.2 us; the launch traced here: 94 us
  Pallas kernels  88.5 us (94%)
  local copies, waits for them, and re-layouts  4.74 us (5%)
    pallas_call x1, Pallas kernels, shards(): pl.pallas_call(kernel, out_shape=(jax.ShapeDtypeStruct((2, TEXT, D), BF16...  88.5 us
    unnamed x17, local copies, waits for them, and re-layouts  2.86 us

profile of v1, /device:TPU:1, one launch (start us, length us, event | category | flops | bytes accessed | tf_op | source)
XLA Modules:
  0.0 94.0 jit_solution(14543567473876472384)
XLA Ops:
  0.6 0.7 reshape.15.gain_in
  1.3 0.0 copy-start.6
  1.3 1.1 %copy.12.text = bf16[2,77,1600]{2,1,0:T(8,128)(2,1)S(1)} copy(bf16[2,77,1600]{2,0,1:T(2,128)(2,1)} %param.12) | data formatting | bytes 985600 | tf_op args[2]
  2.5 0.0 copy-done.6
  2.5 0.0 copy-start
  2.5 0.0 copy-start.1
  2.5 0.0 copy-start.2
  2.5 0.0 copy-start.3
  2.5 0.0 copy-start.4
  2.6 0.0 copy-start.5
  2.6 0.8 copy.13.cot
  3.4 0.0 copy-done
  3.4 0.0 copy-done.1
  3.4 0.0 copy-done.2
  3.4 0.0 copy-done.3
  3.4 0.0 copy-done.4
  3.4 0.0 copy-done.5
  3.5 88.5 %shard_map.113 = (bf16[2,77,1600]{2,1,0:T(8,128)(2,1)S(1)}, bf16[16,16,1024]{2,1,0:T(8,128)(2,1)S(1)}) custom-call(bf16[512,1024]{1,0:T(8,128)(2,1)} %bitcast.3, bf16[16,32]{1,0:T(8,128)(2,1)S(1)} %bitcast.2, bf16[2,77,1600]{2,1,0:T(8,128)(2,1)S(1)} %copy.12.text, f32[1,1600]{1,0:T(1,128)S(1)} %reshape.15.gain_in, s32[2]{0:T(128)S(1)} %copy-done.5, ...), custom_call_target="tpu_custom_call" | custom-call | tf_op jit(solution)/shard_map/pallas_call | solution.py:403
  92.0 1.2 %copy.14 = bf16[2,77,1600]{2,0,1:T(2,128)(2,1)} copy(bf16[2,77,1600]{2,1,0:T(8,128)(2,1)S(1)} %get-tuple-element.2) | data formatting | bytes 985600 | tf_op jit(solution)/shard_map/pallas_call | solution.py:403
  93.2 0.8 copy.16
Async XLA Ops:
  1.3 1.2 %copy-start.6 = (bf16[2,77,1600]{2,0,1:T(2,128)(2,1)S(1)}, bf16[2,77,1600]{2,0,1:T(2,128)(2,1)}, u32[]{:S(2)}) copy-start(bf16[2,77,1600]{2,0,1:T(2,128)(2,1)} %param.15) | copy-start | bytes 1478404
  2.5 0.9 copy-start
  2.5 0.9 copy-start.1
  2.5 0.9 copy-start.2
  2.5 0.9 copy-start.3
  2.5 0.9 copy-start.4
  2.6 0.9 copy-start.5

commit v2 on v1

v2 whole, which is shorter than its diff:
```python
import functools

import jax
import jax.numpy as jnp
from jax import lax
from jax.experimental import pallas as pl
from jax.experimental.pallas import tpu as pltpu
from jax.sharding import PartitionSpec as P

HD = 64
EPSILON = 1e-05
MESH = pl.DeviceIdType.MESH
F32 = jnp.float32
BF16 = jnp.bfloat16

D = 1600
DP = 1664
V = 1024
HW = 896
TEXT = 77
TP = 80
QL = 1408
OL = 1536
LAT = 16
FRAMES = 8
ROWS = 2 * TP


def dot(left, right):
    return jnp.dot(left, right, preferred_element_type=F32)


def dot_nt(left, right):
    return lax.dot_general(left, right, (((1,), (1,)), ((), ())), preferred_element_type=F32)


def dot_tn(left, right):
    return lax.dot_general(left, right, (((0,), (0,)), ((), ())), preferred_element_type=F32)


def kernel(
    video, pool_w, text, gain_in, lengths, cot, q_in, k_in, v_in, o_in,
    grad_text, grad_pooled,
    qb, ob, kb, vb, qw, ow, qf, of, qs, os_, xs, cs, gain, unit, normed, go, queries, ga,
    pooled, lat, kl, vl, gk, gv, gq, back,
    send, recv, cross_send, cross_recv, pool_send, pool_recv, back_send, back_recv, own_sem, in_sem, text_in, cot_in, video_in, q_own, o_own, probs_all,
):
    dp = lax.axis_index("dp")
    f = lax.axis_index("frame")
    y, x, h, c = dp // 16, (dp // 4) % 4, (dp // 2) % 2, dp % 2
    o = 1 - h

    def device(y, x, h, c, f):
        return (((y * 4 + x) * 2 + h) * 2 + c, f)

    def up(i):
        return (i + 1) % 4

    def down(i):
        return (i + 3) % 4

    def far(i):
        return (i + 2) % 4

    sibling = device(y, x, h, 1 - c, f)
    x_up, x_down = device(y, up(x), h, c, f), device(y, down(x), h, c, f)
    y_up, y_down = device(up(y), x, h, c, f), device(down(y), x, h, c, f)

    x_far, y_far = device(y, far(x), h, c, f), device(far(y), x, h, c, f)

    def spread_rows(ref, t, pair):
        for j in range(12):
            ref[j, 2 * t:2 * t + 2, :] = pair[:, 128 * j:128 * j + 128]
        ref[12, 2 * t:2 * t + 2, 0:64] = pair[:, 1536:D]

    def clip_rows(ref, clip):
        return jnp.concatenate([ref[j, pl.ds(clip, TP, stride=2), :] for j in range(13)], axis=1)

    barrier = pltpu.get_barrier_semaphore()

    def greet(who):
        pl.semaphore_signal(barrier, inc=1, device_id=who, device_id_type=MESH)

    for who in (sibling, x_up, x_down, x_far, y_up, y_down, y_far):
        greet(who)
    for step in range(1, FRAMES):
        greet((dp, (f + step) % FRAMES))
    other_dp = device(y, x, o, c, f)[0]
    at_low = f == 0
    at_high = f == FRAMES - 1
    at_end = jnp.logical_or(at_low, at_high)

    @pl.when(at_low)
    def _():
        for k in range(4):
            greet((other_dp, 7 - k))

    @pl.when(at_high)
    def _():
        for k in range(4):
            greet((other_dp, k))

    @pl.when(jnp.logical_not(at_end))
    def _():
        greet((other_dp, jnp.where(f < 4, FRAMES - 1, 0)))

    k_copy = pltpu.make_async_copy(k_in, kb.at[y, x, h, c], in_sem.at[5])
    v_copy = pltpu.make_async_copy(v_in, vb.at[y, x, h, c], in_sem.at[6])
    q_copy = pltpu.make_async_copy(q_in, q_own, in_sem.at[3])
    o_copy = pltpu.make_async_copy(o_in, o_own, in_sem.at[4])
    for coming in (o_copy, q_copy, k_copy, v_copy):
        coming.start()
    video_copy = pltpu.make_async_copy(video, video_in, in_sem.at[0])
    video_copy.start()
    text_copy = pltpu.make_async_copy(text, text_in, in_sem.at[1])
    text_copy.start()
    cot_copy = pltpu.make_async_copy(cot, cot_in, in_sem.at[2])
    cot_copy.start()

    qs[...] = jnp.zeros_like(qs)
    os_[...] = jnp.zeros_like(os_)
    o_copy.wait()
    q_copy.wait()
    q = q_own[...].astype(F32)
    qs[:, 0:HW] = q[0:16]
    qs[0:8, HW:QL] = q[16:24, 0:512]
    qs[8:16, HW:HW + 384] = q[16:24, 512:HW]
    for b in range(7):
        qs[8 + b:9 + b, HW + 384:QL] = q[24:25, 128 * b:128 * b + 128]
    qb[y, x, h, c] = qs[...].astype(BF16)
    rest = o_own[...].astype(F32)
    os_[0:14, :] = rest[:, 0:OL]
    for b in range(7):
        os_[14:16, 128 * b:128 * b + 64] = rest[2 * b:2 * b + 2, OL:D]
    ob[y, x, h, c] = os_[...].astype(BF16)
    k_copy.wait()
    v_copy.wait()

    count = 14 + jnp.where(at_end, 4, 1)
    pl.semaphore_wait(barrier, count)

    bufs = (qb, ob, kb, vb)
    x_first = (True, False, False, True)
    sends = []

    def copy(src, dst, s_sem, r_sem, who):
        return pltpu.make_async_remote_copy(
            src_ref=src, dst_ref=dst, send_sem=s_sem, recv_sem=r_sem, device_id=who,
            device_id_type=MESH)

    def parts(w):
        buf = bufs[w]
        if x_first[w]:
            return (
                lambda a, z: buf.at[y, a, z, c],
                lambda b, z: buf.at[b, :, z, c],
                lambda b, z, k: buf.at[b, pl.ds(2 * k, 2), z, c],
                (lambda b, z: buf.at[b, :, z, 1 - c]),
                x, y, x_up, x_down, x_far, y_up, y_down,
            )
        return (
            lambda a, z: buf.at[a, x, z, c],
            lambda b, z: buf.at[:, b, z, c],
            lambda b, z, k: buf.at[pl.ds(2 * k, 2), b, z, c],
            (lambda b, z: buf.at[:, b, z, 1 - c]),
            y, x, y_up, y_down, y_far, x_up, x_down,
        )

    def step(w, s, k):
        item, row, pair, other_row, a, b, a_up, a_down, a_far, b_up, b_down = parts(w)
        z = h if s == 0 else o

        def go_(ref, index, who):
            moving = copy(ref, ref, send.at[w, s, index], recv.at[w, s, index], who)
            moving.start()
            sends.append(moving)

        def come(ref, index, who):
            copy(ref, ref, send.at[w, s, index], recv.at[w, s, index], who).wait_recv()

        if k == 0:
            if s == 1:
                mine = bufs[w].at[y, x, o, c]
                copy(mine, mine, cross_send.at[w, 0], cross_recv.at[w], (other_dp, f)).wait_recv()
            go_(item(a, z), 0, a_up)
            go_(item(a, z), 1, a_down)
            go_(item(a, z), 2, a_far)
        elif k == 1:
            come(item(down(a), z), 0, a_up)
            come(item(up(a), z), 1, a_down)
            come(item(far(a), z), 2, a_far)
            go_(pair(b, z, 0), 3, b_up)
            go_(pair(b, z, 1), 6, b_down)
            go_(row(b, z), 9, sibling)
        elif k == 2:
            come(pair(down(b), z, 0), 3, b_up)
            go_(pair(down(b), z, 0), 7, b_up)
            come(pair(up(b), z, 1), 6, b_down)
            go_(pair(up(b), z, 1), 8, b_down)
            go_(pair(b, z, 1), 4, b_up)
            go_(pair(b, z, 0), 5, b_down)
        elif k == 3:
            come(pair(down(b), z, 1), 4, b_up)
            go_(row(down(b), z), 10, sibling)
            come(pair(up(b), z, 0), 5, b_down)
            go_(row(up(b), z), 11, sibling)
            come(pair(far(b), z, 0), 7, b_up)
            come(pair(far(b), z, 1), 8, b_down)
            go_(row(far(b), z), 12, sibling)
        else:
            for n, at in enumerate((b, down(b), up(b), far(b))):
                ref = other_row(at, z)
                copy(ref, ref, send.at[w, s, 9 + n], recv.at[w, s, 9 + n], sibling).wait_recv()

    def steps(k, s, *which):
        for w in which:
            step(w, s, k)

    steps(0, 0, 0, 2)

    def cross(where, k, w, target):
        mine = bufs[w].at[y, x, h, c]
        return copy(mine, mine, cross_send.at[w, k], cross_recv.at[w], (other_dp, target))

    def start_cross(which):
        @pl.when(at_low)
        def _():
            for w in which:
                for k in range(4):
                    cross(0, k, w, 4 + k).start()

        @pl.when(at_high)
        def _():
            for w in which:
                for k in range(4):
                    cross(1, k, w, 3 - k).start()

    start_cross((0, 2))
    steps(0, 0, 3, 1)

    i0 = lax.broadcasted_iota(jnp.int32, (32, 256), 0)
    i1 = lax.broadcasted_iota(jnp.int32, (32, 256), 1)
    spread = jnp.where(i1 % 32 == i0, 1.0, 0.0).astype(BF16)
    wide = dot(pool_w[...], spread)
    wide = jnp.concatenate([wide] * 8, axis=0)
    j0 = lax.broadcasted_iota(jnp.int32, (128, 256), 0)
    j1 = lax.broadcasted_iota(jnp.int32, (128, 256), 1)
    diag = jnp.where(j0 // 16 == j1 // 32, wide, 0.0).astype(BF16)
    video_copy.wait()
    for half in range(2):
        part = dot(diag, video_in[256 * half:256 * half + 256, :])
        pooled[128 * half:128 * half + 128, :] = part.astype(BF16)

    def pool_copy(clip, to, frm):
        start = pl.multiple_of(32 * to + 16 * clip, 16)
        place = pl.multiple_of(16 * frm, 16)
        return copy(
            pooled.at[pl.ds(start, 16), :], lat.at[clip, pl.ds(place, 16), :],
            pool_send.at[clip, to], pool_recv.at[clip, frm], (dp, to))

    for clip in range(2):
        for n in range(1, FRAMES):
            pool_copy(clip, (f + n) % FRAMES, f).start()
        start = pl.multiple_of(32 * f + 16 * clip, 16)
        place = pl.multiple_of(16 * f, 16)
        lat[clip, pl.ds(place, 16), :] = pooled[pl.ds(start, 16), :]

    steps(1, 0, 2, 0, 3, 1)
    start_cross((3, 1))
    gain[...] = jnp.zeros_like(gain)
    gain[0:1, 0:D] = gain_in[...].reshape(1, D)
    xs[...] = jnp.zeros_like(xs)
    text_copy.wait()
    for t in range(TEXT):
        spread_rows(xs, t, text_in[t].astype(F32))
    steps(2, 0, 2, 0)
    cs[...] = jnp.zeros_like(cs)
    cot_copy.wait()
    for t in range(TEXT):
        spread_rows(cs, t, cot_in[t].astype(F32))
    steps(2, 0, 3, 1)
    steps(0, 1, 2, 0)
    lane = lax.broadcasted_iota(jnp.int32, (TP, DP), 1)
    position = lax.broadcasted_iota(jnp.int32, (TP, DP), 0)
    inverses = []
    for clip in range(2):
        rows = slice(TP * clip, TP * clip + TP)
        states = clip_rows(xs, clip)
        average = jnp.sum(states, axis=1, keepdims=True) * (1.0 / D)
        centered = jnp.where(lane < D, states - average, 0.0)
        square = jnp.sum(centered * centered, axis=1, keepdims=True) * (1.0 / D)
        inverse = lax.rsqrt(square + EPSILON)
        inverses.append(inverse)
        unit_rows = centered * inverse
        unit[rows, :] = unit_rows
        normed[rows, :] = (unit_rows * gain[0:1, :]).astype(BF16)
        go[rows, :] = jnp.where(position < lengths[clip], clip_rows(cs, clip), 0.0).astype(BF16)
        if clip == 0:
            steps(0, 1, 3, 1)
    steps(1, 1, 2, 0)
    steps(3, 0, 2, 0, 3, 1)
    steps(1, 1, 3, 1)
    steps(2, 1, 2, 0)

    qw[D:DP, :] = jnp.zeros((DP - D, HW), BF16)

    of[...] = jnp.zeros_like(of)

    def unpack_q(zz):
        def body(j, carry):
            for xx in range(4):
                for cc in range(2):
                    at = 25 * (4 * xx + 2 * zz + cc)
                    t = qb[j, xx, zz, cc].astype(F32)
                    qf[j, at:at + 16, :] = t[:, 0:HW]
                    qf[j, at + 16:at + 24, 0:512] = t[0:8, HW:QL]
                    qf[j, at + 16:at + 24, 512:HW] = t[8:16, HW:HW + 384]
                    for b in range(7):
                        qf[j, at + 24:at + 25, 128 * b:128 * b + 128] = t[8 + b:9 + b, HW + 384:QL]
            return carry

        lax.fori_loop(0, 4, body, 0)

    def unpack_o(zz):
        def body(j, carry):
            for xx in range(4):
                for cc in range(2):
                    at = 14 * (4 * xx + 2 * zz + cc)
                    t = ob[j, xx, zz, cc].astype(F32)
                    of[j, at:at + 14, 0:OL] = t[0:14]
                    for b in range(7):
                        of[j, at + 2 * b:at + 2 * b + 2, OL:D] = t[14:16, 128 * b:128 * b + 64]
            return carry

        lax.fori_loop(0, 4, body, 0)

    def unpack_part(unpack, mine):
        for zz in range(2):
            @pl.when((h == zz) if mine else (h != zz))
            def _(zz=zz):
                unpack(zz)

    steps(4, 0, 0)
    unpack_part(unpack_q, True)
    steps(2, 1, 3, 1)
    steps(4, 0, 1)
    unpack_part(unpack_o, True)
    steps(3, 1, 2, 0)
    steps(4, 0, 2)
    steps(4, 1, 2, 0)
    unpack_part(unpack_q, False)
    for j in range(4):
        qw[400 * j:400 * j + 400, :] = qf[j].astype(BF16)
    queries[...] = dot(normed[...], qw[...]).astype(BF16)

    for clip in range(2):
        for n in range(1, FRAMES):
            frm = (f + n) % FRAMES
            place = pl.multiple_of(16 * frm, 16)
            got = lat.at[clip, pl.ds(place, 16), :]
            copy(got, got, pool_send.at[clip, frm], pool_recv.at[clip, frm], (dp, frm)).wait_recv()

    kl[...] = dot(lat[...].reshape(256, V), kb[...].reshape(V, HW)).astype(BF16)

    low = lax.broadcasted_iota(jnp.int32, (128, 128), 1) < HD
    scale = HD ** -0.5
    zero = jnp.zeros((128, 128), BF16)

    def split(block):
        return jnp.concatenate([jnp.where(low, block, zero), jnp.where(low, zero, block)], axis=0)

    for clip in range(2):
        rows = slice(TP * clip, TP * clip + TP)
        lats = slice(128 * clip, 128 * clip + 128)
        for p in range(7):
            cols = slice(128 * p, 128 * p + 128)
            scores = dot_nt(split(kl[lats, cols]), queries[rows, cols]).reshape(2, 128, TP) * scale
            top = jnp.max(scores, axis=1, keepdims=True)
            shifted = jnp.exp(scores - top)
            probs_all[7 * clip + p] = shifted / jnp.sum(shifted, axis=1, keepdims=True)

    steps(3, 1, 3, 1)
    steps(4, 0, 3)
    steps(4, 1, 1)
    unpack_part(unpack_o, False)
    for j in range(4):
        ow[224 * j:224 * j + 224, :] = of[j].astype(BF16)
    ga[...] = dot_nt(go[...], ow[...]).astype(BF16)
    steps(4, 1, 3)
    key_w = kb[...].reshape(V, HW)
    value_w = vb[...].reshape(V, HW)
    vl[...] = dot(lat[...].reshape(256, V), value_w).astype(BF16)

    def back_copy(clip, to, frm):
        rows = pl.multiple_of(16 * to, 16)
        return copy(
            back.at[clip, pl.ds(rows, 16), :], grad_pooled.at[2 * frm + clip],
            back_send.at[clip, to], back_recv.at[clip, frm], (dp, to))

    for clip in range(2):
        rows = slice(TP * clip, TP * clip + TP)
        lats = slice(128 * clip, 128 * clip + 128)
        for p in range(7):
            cols = slice(128 * p, 128 * p + 128)
            qp = queries[rows, cols]
            gp = ga[rows, cols]
            kd = split(kl[lats, cols])
            vd = split(vl[lats, cols])
            grad_probs = dot_nt(vd, gp).reshape(2, 128, TP)
            probs = probs_all[7 * clip + p]
            probs_low = probs.astype(BF16)
            row_term = jnp.sum(probs_low.astype(F32) * grad_probs, axis=1, keepdims=True)
            grad_scores = (probs * (grad_probs - row_term) * scale).astype(BF16).reshape(256, TP)
            dk = dot(grad_scores, qp)
            dv = dot(probs_low.reshape(256, TP), gp)
            gk[lats, cols] = jnp.where(low, dk[0:128], dk[128:256]).astype(BF16)
            gv[lats, cols] = jnp.where(low, dv[0:128], dv[128:256]).astype(BF16)
            gq[rows, cols] = dot_tn(grad_scores, kd).astype(BF16)
        result = dot_nt(gk[lats, :], key_w) + dot_nt(gv[lats, :], value_w)
        back[clip] = result.astype(BF16)
        for n in range(1, FRAMES):
            back_copy(clip, (f + n) % FRAMES, f).start()
        mine = pl.multiple_of(16 * f, 16)
        pltpu.make_async_copy(
            back.at[clip, pl.ds(mine, 16), :], grad_pooled.at[2 * f + clip], own_sem.at[clip]
        ).start()

    grad_normed = dot_nt(gq[...], qw[...])
    for clip in range(2):
        rows = slice(TP * clip, TP * clip + TP)
        g = grad_normed[rows] * gain[0:1, :]
        unit_rows = unit[rows, :]
        mean_g = jnp.sum(g, axis=1, keepdims=True) * (1.0 / D)
        mean_gu = jnp.sum(g * unit_rows, axis=1, keepdims=True) * (1.0 / D)
        out = inverses[clip] * (g - mean_g - unit_rows * mean_gu)
        for j in range(13):
            xs[j, pl.ds(clip, TP, stride=2), :] = out[:, 128 * j:128 * j + 128]
    for t in range(TEXT):
        both = jnp.concatenate([xs[j, 2 * t:2 * t + 2, :] for j in range(13)], axis=1)
        grad_text[t] = both[:, 0:D].astype(BF16)

    for moving in sends:
        moving.wait_send()
    for clip in range(2):
        for n in range(1, FRAMES):
            to = (f + n) % FRAMES
            pool_copy(clip, to, f).wait_send()
            back_copy(clip, to, f).wait_send()
        for n in range(1, FRAMES):
            frm = (f + n) % FRAMES
            got = grad_pooled.at[2 * frm + clip]
            copy(got, got, back_send.at[clip, frm], back_recv.at[clip, frm], (dp, frm)).wait_recv()
        mine = pl.multiple_of(16 * f, 16)
        pltpu.make_async_copy(
            back.at[clip, pl.ds(mine, 16), :], grad_pooled.at[2 * f + clip], own_sem.at[clip]
        ).wait()

    @pl.when(at_low)
    def _():
        for w in range(4):
            for k in range(4):
                cross(0, k, w, 4 + k).wait_send()

    @pl.when(at_high)
    def _():
        for w in range(4):
            for k in range(4):
                cross(1, k, w, 3 - k).wait_send()


def shards(video, pool_w, text, gain, lengths, cot, q_w, k_w, v_w, o_w):
    vmem = pl.BlockSpec(memory_space=pltpu.VMEM)
    smem = pl.BlockSpec(memory_space=pltpu.SMEM)
    dma = pltpu.SemaphoreType.DMA
    anywhere = pl.BlockSpec(memory_space=pl.ANY)
    grad_text, grad_pooled = pl.pallas_call(
        kernel,
        out_shape=(
            jax.ShapeDtypeStruct((TEXT, 2, D), BF16),
            jax.ShapeDtypeStruct((16, LAT, V), BF16),
        ),
        in_specs=[anywhere, vmem, anywhere, vmem, smem, anywhere, anywhere, anywhere, anywhere, anywhere],
        out_specs=(vmem, anywhere),
        scratch_shapes=[
            pltpu.VMEM((4, 4, 2, 2, 16, QL), BF16),
            pltpu.VMEM((4, 4, 2, 2, 16, OL), BF16),
            pltpu.VMEM((4, 4, 2, 2, 16, HW), BF16),
            pltpu.VMEM((4, 4, 2, 2, 16, HW), BF16),
            pltpu.VMEM((DP, HW), BF16),
            pltpu.VMEM((HW, DP), BF16),
            pltpu.VMEM((4, 400, HW), F32),
            pltpu.VMEM((4, 224, DP), F32),
            pltpu.VMEM((16, QL), F32),
            pltpu.VMEM((16, OL), F32),
            pltpu.VMEM((13, ROWS, 128), F32),
            pltpu.VMEM((13, ROWS, 128), F32),
            pltpu.VMEM((8, DP), F32),
            pltpu.VMEM((ROWS, DP), F32),
            pltpu.VMEM((ROWS, DP), BF16),
            pltpu.VMEM((ROWS, DP), BF16),
            pltpu.VMEM((ROWS, HW), BF16),
            pltpu.VMEM((ROWS, HW), BF16),
            pltpu.VMEM((256, V), BF16),
            pltpu.VMEM((2, 128, V), BF16),
            pltpu.VMEM((256, HW), BF16),
            pltpu.VMEM((256, HW), BF16),
            pltpu.VMEM((256, HW), BF16),
            pltpu.VMEM((256, HW), BF16),
            pltpu.VMEM((ROWS, HW), BF16),
            pltpu.VMEM((2, 128, V), BF16),
            dma((4, 2, 13)),
            dma((4, 2, 13)),
            dma((4, 4)),
            dma((4,)),
            dma((2, FRAMES)),
            dma((2, FRAMES)),
            dma((2, FRAMES)),
            dma((2, FRAMES)),
            dma((2,)),
            dma((7,)),
            pltpu.VMEM((TEXT, 2, D), BF16),
            pltpu.VMEM((TEXT, 2, D), BF16),
            pltpu.VMEM((512, V), BF16),
            pltpu.VMEM((25, HW), BF16),
            pltpu.VMEM((14, D), BF16),
            pltpu.VMEM((14, 2, 128, TP), F32),
        ],
        compiler_params=pltpu.CompilerParams(
            collective_id=0, has_side_effects=True, vmem_limit_bytes=60 * 1024 * 1024
        ),
    )(
        video.reshape(512, V), pool_w.reshape(LAT, 32), text.transpose(1, 0, 2), gain, lengths,
        cot.transpose(1, 0, 2), q_w, k_w, v_w, o_w,
    )
    return grad_text.transpose(1, 0, 2), grad_pooled


def solution(mesh):
    both = ("dp", "frame")
    return jax.shard_map(
        shards,
        mesh=mesh,
        in_specs=(
            P("dp", "frame", None, None), P("frame", None, None), P(both, None, None), P(), P(both),
            P(both, None, None), P("dp", None), P("dp", None), P("dp", None), P("dp", None),
        ),
        out_specs=(P(both, None, None), P("dp", "frame", None)),
        check_vma=False,
    )
```

time: 94.2 us -> 86.1 us (0.914)
  Pallas kernels: 88.5 us -> 81.6 us
  local copies, waits for them, and re-layouts: 4.74 us -> 3.03 us
    pallas_call x1, Pallas kernels: 88.5 us -> 81.6 us  [shards(): pl.pallas_call(kernel, out_shape=(jax.ShapeDtypeStruct((TEXT, 2, D), BF16...]
    pallas_call x1 -> x0, local copies, waits for them, and re-layouts: 1.18 us -> none  [shards(): pl.pallas_call(kernel, out_shape=(jax.ShapeDtypeStruct((2, TEXT, D), BF16...]
    unnamed x17 -> x4, local copies, waits for them, and re-layouts: 2.86 us -> 3.03 us
where the time goes in v2:
time: 86.1 us; the launch traced here: 85.3 us
  Pallas kernels  81.6 us (95%)
  local copies, waits for them, and re-layouts  3.03 us (4%)
    pallas_call x1, Pallas kernels, shards(): pl.pallas_call(kernel, out_shape=(jax.ShapeDtypeStruct((TEXT, 2, D), BF16...  81.6 us
    unnamed x4, local copies, waits for them, and re-layouts  3.03 us

profile of v2, /device:TPU:1, one launch (start us, length us, event | category | flops | bytes accessed | tf_op | source)
XLA Modules:
  0.0 85.3 jit_solution(11446042717252610689)
XLA Ops:
  0.6 81.6 %shard_map.113 = (bf16[77,2,1600]{2,1,0:T(2,128)(2,1)}, bf16[16,16,1024]{2,1,0:T(8,128)(2,1)}) custom-call(bf16[512,1024]{1,0:T(8,128)(2,1)} %bitcast.5, bf16[16,32]{1,0:T(8,128)(2,1)} %bitcast.9, bf16[77,2,1600]{2,1,0:T(2,128)(2,1)} %bitcast.6, f32[1600]{0:T(1024)} %gain_in.1, s32[2]{0:T(128)} %lengths.1, bf16[77,2,1600]{2,1,0:T(2,128)(2,1)} %bitcast.7, ...), custom_call_target="tpu_custom_call" | custom-call | tf_op jit(solution)/shard_map/pallas_call | solution.py:476
  82.3 0.0 copy-start
  82.3 2.2 %copy.14 = bf16[2,77,1600]{2,0,1:T(2,128)(2,1)} copy(bf16[2,77,1600]{2,0,1:T(2,128)(2,1)} %bitcast.8) | data formatting | bytes 985600
  84.5 0.0 copy-done
  84.5 0.8 copy.15
Async XLA Ops:
  82.3 2.2 %copy-start = (bf16[16,16,1024]{2,1,0:T(8,128)(2,1)S(1)}, bf16[16,16,1024]{2,1,0:T(8,128)(2,1)}, u32[]{:S(2)}) copy-start(bf16[16,16,1024]{2,1,0:T(8,128)(2,1)} %get-tuple-element.9) | copy-start | bytes 1572868

commit v3 on v2

--- a/solution.py
+++ b/solution.py
@@ -155,19 +155,21 @@
                 lambda a, z: buf.at[y, a, z, c],
                 lambda b, z: buf.at[b, :, z, c],
                 lambda b, z, k: buf.at[b, pl.ds(2 * k, 2), z, c],
-                (lambda b, z: buf.at[b, :, z, 1 - c]),
+                lambda b, z: buf.at[b, :, z, 1 - c],
+                lambda b, z, k: buf.at[b, pl.ds(2 * k, 2), z, 1 - c],
                 x, y, x_up, x_down, x_far, y_up, y_down,
             )
         return (
             lambda a, z: buf.at[a, x, z, c],
             lambda b, z: buf.at[:, b, z, c],
             lambda b, z, k: buf.at[pl.ds(2 * k, 2), b, z, c],
-            (lambda b, z: buf.at[:, b, z, 1 - c]),
+            lambda b, z: buf.at[:, b, z, 1 - c],
+            lambda b, z, k: buf.at[pl.ds(2 * k, 2), b, z, 1 - c],
             y, x, y_up, y_down, y_far, x_up, x_down,
         )
 
     def step(w, s, k):
-        item, row, pair, other_row, a, b, a_up, a_down, a_far, b_up, b_down = parts(w)
+        item, row, pair, other_row, other_pair, a, b, a_up, a_down, a_far, b_up, b_down = parts(w)
         z = h if s == 0 else o
 
         def go_(ref, index, who):
@@ -199,17 +201,22 @@
             go_(pair(up(b), z, 1), 8, b_down)
             go_(pair(b, z, 1), 4, b_up)
             go_(pair(b, z, 0), 5, b_down)
+            go_(pair(down(b), z, 0), 10, sibling)
+            go_(pair(up(b), z, 1), 11, sibling)
         elif k == 3:
             come(pair(down(b), z, 1), 4, b_up)
-            go_(row(down(b), z), 10, sibling)
+            go_(pair(down(b), z, 1), 12, sibling)
             come(pair(up(b), z, 0), 5, b_down)
-            go_(row(up(b), z), 11, sibling)
+            go_(pair(up(b), z, 0), 13, sibling)
             come(pair(far(b), z, 0), 7, b_up)
+            go_(pair(far(b), z, 0), 14, sibling)
             come(pair(far(b), z, 1), 8, b_down)
-            go_(row(far(b), z), 12, sibling)
+            go_(pair(far(b), z, 1), 15, sibling)
         else:
-            for n, at in enumerate((b, down(b), up(b), far(b))):
-                ref = other_row(at, z)
+            refs = (other_row(b, z), other_pair(down(b), z, 0), other_pair(up(b), z, 1),
+                    other_pair(down(b), z, 1), other_pair(up(b), z, 0),
+                    other_pair(far(b), z, 0), other_pair(far(b), z, 1))
+            for n, ref in enumerate(refs):
                 copy(ref, ref, send.at[w, s, 9 + n], recv.at[w, s, 9 + n], sibling).wait_recv()
 
     def steps(k, s, *which):
@@ -251,6 +258,8 @@
         part = dot(diag, video_in[256 * half:256 * half + 256, :])
         pooled[128 * half:128 * half + 128, :] = part.astype(BF16)
 
+    start_cross((3, 1))
+
     def pool_copy(clip, to, frm):
         start = pl.multiple_of(32 * to + 16 * clip, 16)
         place = pl.multiple_of(16 * frm, 16)
@@ -266,7 +275,6 @@
         lat[clip, pl.ds(place, 16), :] = pooled[pl.ds(start, 16), :]
 
     steps(1, 0, 2, 0, 3, 1)
-    start_cross((3, 1))
     gain[...] = jnp.zeros_like(gain)
     gain[0:1, 0:D] = gain_in[...].reshape(1, D)
     xs[...] = jnp.zeros_like(xs)
@@ -466,6 +474,11 @@
         for w in range(4):
             for k in range(4):
                 cross(1, k, w, 3 - k).wait_send()
+
+
+def settle(text_in, pooled_in, text_out, pooled_out):
+    pooled_out[...] = pooled_in[...]
+    text_out[...] = text_in[...]
 
 
 def shards(video, pool_w, text, gain, lengths, cot, q_w, k_w, v_w, o_w):
@@ -508,8 +521,8 @@
             pltpu.VMEM((256, HW), BF16),
             pltpu.VMEM((ROWS, HW), BF16),
             pltpu.VMEM((2, 128, V), BF16),
-            dma((4, 2, 13)),
-            dma((4, 2, 13)),
+            dma((4, 2, 16)),
+            dma((4, 2, 16)),
             dma((4, 4)),
             dma((4,)),
             dma((2, FRAMES)),
@@ -532,6 +545,15 @@
         video.reshape(512, V), pool_w.reshape(LAT, 32), text.transpose(1, 0, 2), gain, lengths,
         cot.transpose(1, 0, 2), q_w, k_w, v_w, o_w,
     )
+    grad_text, grad_pooled = pl.pallas_call(
+        settle,
+        out_shape=(
+            jax.ShapeDtypeStruct((TEXT, 2, D), BF16),
+            jax.ShapeDtypeStruct((16, LAT, V), BF16),
+        ),
+        in_specs=[vmem, vmem],
+        out_specs=(vmem, vmem),
+    )(grad_text, grad_pooled)
     return grad_text.transpose(1, 0, 2), grad_pooled
 
 

time: 86.1 us -> 85.3 us (level)
  local copies, waits for them, and re-layouts: 3.03 us -> 0 us
  Pallas kernels: 81.6 us -> 83.9 us
    unnamed x4 -> x0, local copies, waits for them, and re-layouts: 3.03 us -> none
    pallas_call x0 -> x1, Pallas kernels: none -> 2.19 us  [shards(): pl.pallas_call(settle, out_shape=(jax.ShapeDtypeStruct((TEXT, 2, D), BF16...]
where the time goes in v3:
time: 85.3 us; the launch traced here: 84.5 us
  Pallas kernels  83.9 us (98%)
    pallas_call x1, Pallas kernels, shards(): pl.pallas_call(kernel, out_shape=(jax.ShapeDtypeStruct((TEXT, 2, D), BF16...  81.7 us
    pallas_call x1, Pallas kernels, shards(): pl.pallas_call(settle, out_shape=(jax.ShapeDtypeStruct((TEXT, 2, D), BF16...  2.19 us

profile of v3, /device:TPU:1, one launch (start us, length us, event | category | flops | bytes accessed | tf_op | source)
XLA Modules:
  0.0 84.5 jit_solution(16800712348084559656)
XLA Ops:
  0.6 81.7 %shard_map.113 = (bf16[77,2,1600]{2,1,0:T(2,128)(2,1)}, bf16[16,16,1024]{2,1,0:T(8,128)(2,1)}) custom-call(bf16[512,1024]{1,0:T(8,128)(2,1)} %bitcast.5, bf16[16,32]{1,0:T(8,128)(2,1)} %bitcast.8, bf16[77,2,1600]{2,1,0:T(2,128)(2,1)} %bitcast.6, f32[1600]{0:T(1024)} %gain_in.1, s32[2]{0:T(128)} %lengths.1, bf16[77,2,1600]{2,1,0:T(2,128)(2,1)} %bitcast.7, ...), custom_call_target="tpu_custom_call" | custom-call | tf_op jit(solution)/shard_map/pallas_call | solution.py:489
  82.3 2.2 %shard_map.114 = (bf16[77,2,1600]{2,1,0:T(2,128)(2,1)}, bf16[16,16,1024]{2,1,0:T(8,128)(2,1)}) custom-call(bf16[77,2,1600]{2,1,0:T(2,128)(2,1)} %get-tuple-element.6.text_in, bf16[16,16,1024]{2,1,0:T(8,128)(2,1)} %get-tuple-element.7.pooled_in), custom_call_target="tpu_custom_call" | custom-call | tf_op jit(solution)/shard_map/pallas_call | solution.py:548
